TPU v7x, 256 devices: a whole 4x4x8 slice. The times are simulated.
256 devices in a mesh: dp: 32 (over y_lo, z, core), head: 8 (over y_hi, x).
Axes of the slice: x: 4, y: 4 (y_hi: 2, y_lo: 2; y = y_hi * 2 + y_lo), z: 8, core: 2. Of those that a mesh axis runs over, the one named last changes fastest.
Arguments:
- queries: bfloat16 [32, 2048, 2048], P('dp', 'head'), may hold values from -6 to 6
- key_states: bfloat16 [32, 2048, 2048], P('dp', 'head'), may hold values from -6 to 6
- value_states: bfloat16 [32, 2048, 2048], P('dp', 'head'), may hold values from -6 to 6
- queries_dot: bfloat16 [32, 2048, 2048], P('dp', 'head'), may hold values from -6 to 6
- keys_dot: bfloat16 [32, 2048, 2048], P('dp', 'head'), may hold values from -6 to 6
- values_dot: bfloat16 [32, 2048, 2048], P('dp', 'head'), may hold values from -6 to 6
- velocity: bfloat16 [32, 2048, 3072], P('dp', 'head'), may hold values from -3 to 3
- time_gap: float32 [32], P('dp'), may hold values from 0.3 to 1
- merge_slot: int32 [32, 2048], P('dp', 'head'), may hold values from 0 to 127, as said below
- out_weight: bfloat16 [3072, 2048], P(('dp', 'head')), may hold values from -0.125 to 0.125
Outputs:
- grad_attn: bfloat16 [32, 1024, 2048], P('dp', None, 'head')
- grad_weight: float32 [3072, 2048], P('dp', 'head')
Inputs may be any that keep to these rules, and one draw needn't show every extreme that they name: `merge_slot`: within each aligned block of 256 source tokens of a clip the values name merged tokens of that block; the source at position 2 m of a block names m, so every merged token has at least one source.
All inputs are finite; a program needn't handle non-finite values.
Results may differ from a plain program's by a relative error of at most 0.0075.
Values may be sent and summed in bfloat16 or wider, within the bound.
A program may use at most 128 MiB of HBM per device.

v0:
```python
import math

import jax
import jax.numpy as jnp
from jax import lax
from jax.sharding import PartitionSpec as P

HD = 128


def attend(queries, keys_in, values_in, queries_tan, keys_tan, values_tan):
    length = queries.shape[0]
    block = min(512, length)
    scale = 1.0 / math.sqrt(queries.shape[2])

    def one_block(index):
        start = index * block
        query_block = lax.dynamic_slice_in_dim(queries, start, block, 0)
        tangent_block = lax.dynamic_slice_in_dim(queries_tan, start, block, 0)
        scores = (
            jnp.einsum("qhd,khd->hqk", query_block, keys_in, preferred_element_type=jnp.float32)
            * scale
        )
        scores_dot = (
            jnp.einsum("qhd,khd->hqk", tangent_block, keys_in, preferred_element_type=jnp.float32)
            + jnp.einsum("qhd,khd->hqk", query_block, keys_tan, preferred_element_type=jnp.float32)
        ) * scale
        highest = jnp.max(scores, axis=-1, keepdims=True)
        weights = jnp.exp(scores - highest)
        weights = weights / jnp.sum(weights, axis=-1, keepdims=True)
        weights_dot = weights * (scores_dot - jnp.sum(weights * scores_dot, axis=-1, keepdims=True))
        probs = weights.astype(jnp.bfloat16)
        probs_dot = weights_dot.astype(jnp.bfloat16)
        mixed = jnp.einsum("hqk,khd->qhd", probs, values_in, preferred_element_type=jnp.float32)
        mixed_dot = jnp.einsum(
            "hqk,khd->qhd", probs_dot, values_in, preferred_element_type=jnp.float32
        ) + jnp.einsum("hqk,khd->qhd", probs, values_tan, preferred_element_type=jnp.float32)
        return (mixed.astype(jnp.bfloat16), mixed_dot.astype(jnp.bfloat16))

    outputs = lax.map(one_block, jnp.arange(length // block, dtype=jnp.int32))
    return (outputs[0].reshape(queries.shape), outputs[1].reshape(queries.shape))


def heads_attention(pieces):
    squeezed = [piece[:, 0] for piece in pieces]
    mixed, mixed_dot = attend(*squeezed)
    return (mixed[:, None], mixed_dot[:, None])


def on_device(
    queries,
    key_states,
    value_states,
    queries_dot,
    keys_dot,
    values_dot,
    velocity,
    time_gap,
    merge_slot,
    out_weight,
):
    source_count = queries.shape[1]
    merged_count = source_count // 2
    features = queries.shape[2]
    head_groups = lax.axis_size("head")
    heads_here = features // (head_groups * HD)
    group_width = heads_here * HD
    width = out_weight.shape[0] * lax.axis_size("dp") * head_groups
    select = merge_slot[0][None, :] == jnp.arange(merged_count, dtype=jnp.int32)[:, None]
    onehot = select.astype(jnp.bfloat16)
    counts = jnp.sum(select.astype(jnp.float32), axis=1)

    def merge(data):
        summed = jnp.dot(onehot, data[0], preferred_element_type=jnp.float32)
        merged = (summed / counts[:, None]).astype(jnp.bfloat16)
        return merged.reshape(merged_count, head_groups, heads_here, HD)

    merged_q = merge(queries)
    merged_k = merge(key_states)
    merged_v = merge(value_states)
    merged_tq = merge(queries_dot)
    merged_tk = merge(keys_dot)
    merged_tv = merge(values_dot)
    attn_heads, attn_heads_dot = heads_attention(
        (
            lax.all_to_all(merged_q, "head", split_axis=1, concat_axis=0, tiled=True),
            lax.all_to_all(merged_k, "head", split_axis=1, concat_axis=0, tiled=True),
            lax.all_to_all(merged_v, "head", split_axis=1, concat_axis=0, tiled=True),
            lax.all_to_all(merged_tq, "head", split_axis=1, concat_axis=0, tiled=True),
            lax.all_to_all(merged_tk, "head", split_axis=1, concat_axis=0, tiled=True),
            lax.all_to_all(merged_tv, "head", split_axis=1, concat_axis=0, tiled=True),
        )
    )
    clip_tokens = attn_heads.shape[0]
    attn_flat = attn_heads.reshape(clip_tokens, group_width)
    full_weight = lax.all_gather(out_weight, ("dp", "head"), axis=0, tiled=True)
    head_weight = lax.dynamic_slice_in_dim(
        full_weight, lax.axis_index("head") * group_width, group_width, 1
    )
    attn_tok, attn_tok_dot = (
        lax.all_to_all(attn_heads, "head", split_axis=0, concat_axis=1, tiled=True),
        lax.all_to_all(attn_heads_dot, "head", split_axis=0, concat_axis=1, tiled=True),
    )
    weight_groups = full_weight.reshape(width, head_groups, group_width)

    def project(data):
        grouped = data.reshape(merged_count, head_groups, group_width)
        parts = jnp.einsum(
            "tgf,dgf->gtd", grouped, weight_groups, preferred_element_type=jnp.float32
        )
        parts = lax.optimization_barrier(parts.astype(jnp.bfloat16))
        return jnp.sum(parts.astype(jnp.float32), axis=0).astype(jnp.bfloat16)

    proj = project(attn_tok)
    proj_dot = project(attn_tok_dot)
    spread_dims = (((0,), (0,)), ((), ()))
    mean_flow = lax.dot_general(onehot, proj, spread_dims, preferred_element_type=jnp.float32)
    flow_dot = lax.dot_general(onehot, proj_dot, spread_dims, preferred_element_type=jnp.float32)
    residual = mean_flow - (velocity[0].astype(jnp.float32) - time_gap[0] * flow_dot)
    cotangent = jnp.dot(
        select.astype(jnp.float32), residual, precision=lax.Precision.HIGHEST
    ).astype(jnp.bfloat16)
    clip_cotangent = lax.all_gather(cotangent, "head", axis=0, tiled=True)
    grad_attn = jnp.dot(clip_cotangent, head_weight, preferred_element_type=jnp.float32).astype(
        jnp.bfloat16
    )
    grad_weight = lax.psum_scatter(
        lax.dot_general(
            clip_cotangent, attn_flat, (((0,), (0,)), ((), ())), preferred_element_type=jnp.float32
        ),
        "dp",
        scatter_dimension=0,
        tiled=True,
    )
    return (grad_attn[None], grad_weight)


def solution(mesh):
    placed = (
        P("dp", "head", None),
        P("dp", "head", None),
        P("dp", "head", None),
        P("dp", "head", None),
        P("dp", "head", None),
        P("dp", "head", None),
        P("dp", "head", None),
        P("dp"),
        P("dp", "head"),
        P(("dp", "head"), None),
    )
    return jax.shard_map(
        on_device,
        mesh=mesh,
        in_specs=placed,
        out_specs=(P("dp", None, "head"), P("dp", "head")),
        check_vma=False,
    )
```

profile of v0, /device:TPU:5, one launch (start us, length us, event | category | flops | bytes accessed | tf_op | source)
XLA Modules:
  0.0 1029.0 jit_solution(16152511056107606929)
XLA Ops:
  11.3 7.0 all-to-all-start.1
  21.4 6.1 all-to-all-done.1
  27.5 5.9 all-to-all-start.2
  35.3 7.0 all-to-all-done.2
  42.3 6.1 all-to-all-start.4
  51.6 5.9 all-to-all-done.4
  57.5 5.9 all-to-all-start.5
  66.5 5.9 all-to-all-done.5
  72.5 6.1 all-to-all-start.3
  81.7 5.9 all-to-all-done.3
  87.6 6.0 all-to-all-start
  102.7 29.6 %while.12 = (s32[]{:T(128)}, bf16[2,512,2,128]{3,1,2,0:T(8,128)(2,1)}, bf16[2,512,2,128]{3,1,0,2:T(8,128)(2,1)}, s32[2]{0:T(128)S(1)}, bf16[1024,2,128]{2,1,0:T(...) while((s32[]{:T(128)}, ...), condition=%wide.region_5.6_spmd, body=%wide.region_1.5_spmd.sunk | while | flops 1627783168 | bytes 71594352 | solution.py:40
  134.7 6.0 all-to-all-start.6
  143.1 6.3 all-to-all-done.6
  149.3 6.5 all-to-all-start.7
  156.9 7.7 all-to-all-done.7
  165.0 575.0 %all-gather.6.cloned.1.call-done = bf16[256,12,2048]{2,1,0:T(8,128)(2,1)} async-done(((bf16[1,12,2048]{2,1,0:T(8,128)(2,1)}), bf16[256,12,2048]{2,1,0:T(8,128)(2,1)}) %all-gather.6.cloned.1.call-update) | async-done | bytes 12582928 | tf_op jit(solution)/shard_map/all_gather | solution.py:96
  740.0 22.6 %reshape.54 = bf16[3072,8,256]{2,1,0:T(8,128)(2,1)} reshape(bf16[256,12,2048]{2,1,0:T(8,128)(2,1)} %all-gather.6.cloned.1.call-done) | data formatting | bytes 25165824 | tf_op jit(solution)/shard_map/reshape | solution.py:104
  762.6 11.9 %fusion.33 = bf16[8,128,3072]{2,1,0:T(8,128)(2,1)} fusion(bf16[3072,8,256]{2,1,0:T(8,128)(2,1)} %reshape.54, bf16[128,8,256]{2,1,0:T(8,128)(2,1)S(1)} %bitcast.123), kind=kOutput, calls=%fused_computation.35 | convolution fusion | flops 1613758464 | bytes 19398656 | tf_op jit(solution)/shard_map/tgf,dgf->gtd/dot_general | solution.py:108
  780.8 11.9 %fusion.36 = bf16[8,128,3072]{2,1,0:T(8,128)(2,1)} fusion(bf16[3072,8,256]{2,1,0:T(8,128)(2,1)} %reshape.54, bf16[128,8,256]{2,1,0:T(8,128)(2,1)S(1)} %bitcast.124), kind=kOutput, calls=%fused_computation.36 | convolution fusion | flops 1613758464 | bytes 19398656 | tf_op jit(solution)/shard_map/tgf,dgf->gtd/dot_general | solution.py:108
  802.4 97.5 %all-gather.4.cloned.1.call-done = bf16[1024,3072]{1,0:T(8,128)(2,1)} async-done(((bf16[128,3072]{1,0:T(8,128)(2,1)}), bf16[1024,3072]{1,0:T(8,128)(2,1)}) %all-gather.4.cloned.1.call-update) | async-done | bytes 6291472 | tf_op jit(solution)/shard_map/all_gather | solution.py:123
  899.9 6.3 fusion.61
  906.3 20.0 %reshape.58 = bf16[3072,2048]{1,0:T(8,128)(2,1)} reshape(bf16[256,12,2048]{2,1,0:T(8,128)(2,1)} %all-gather.6.cloned.1.call-done) | data formatting | bytes 25165824
  932.1 90.4 %reduce-scatter.2.cloned.1.call-done = f32[96,256]{1,0:T(8,128)} async-done(((f32[3072,256]{1,0:T(8,128)}), f32[96,256]{1,0:T(8,128)}) %reduce-scatter.2.cloned.1.call-update) | async-done | bytes 98320 | tf_op jit(solution)/shard_map/reduce_scatter | solution.py:127
  (103 shorter events, 83.0 us)
Async XLA Ops:
  7.2 11.1 %copy-start.11 = (s32[1,256]{1,0:T(1,128)S(1)}, s32[1,256]{1,0:T(1,128)}, u32[]{:S(2)}) copy-start(s32[1,256]{1,0:T(1,128)} %param.20) | copy-start | bytes 3076
  7.2 732.8 %all-gather.6.cloned.1.call-start = ((), (), s32[]{:S(2)}) async-start(), calls=%async_computation.11 | async-start | bytes 16842752 | tf_op jit(solution)/shard_map/all_gather | solution.py:96
  11.3 22.1 %copy-start.12 = (bf16[1,256,2048]{2,1,0:T(8,128)(2,1)S(1)}, bf16[1,256,2048]{2,1,0:T(8,128)(2,1)}, u32[]{:S(2)}) copy-start(bf16[1,256,2048]{2,1,0:T(8,128)(2,1)} %param.16) | copy-start | bytes 3145732
  11.3 16.2 %all-to-all-start.1 = ((bf16[128,8,2,128]{3,2,0,1:T(2,128)(2,1)}), bf16[128,8,2,128]{3,2,0,1:T(2,128)(2,1)S(1)}, u32[]{:S(2)}, u32[]{:S(2)}) async-start(bf16[128,8,2,128]{3,2,0,1:T(2,128)(2,1)} %copy.89), calls=%async_computation.1 | async-start | bytes 1048576 | tf_op jit(solution)/shard_map/all_to_all | solution.py:87
  27.5 14.8 %all-to-all-start.2 = ((bf16[128,8,2,128]{3,2,0,1:T(2,128)(2,1)}), bf16[128,8,2,128]{3,2,0,1:T(2,128)(2,1)S(1)}, u32[]{:S(2)}, u32[]{:S(2)}) async-start(bf16[128,8,2,128]{3,2,0,1:T(2,128)(2,1)} %copy.90), calls=%async_computation.2 | async-start | bytes 1048576 | tf_op jit(solution)/shard_map/all_to_all | solution.py:88
  42.3 15.2 %all-to-all-start.4 = ((bf16[128,8,2,128]{3,2,0,1:T(2,128)(2,1)}), bf16[128,8,2,128]{3,2,0,1:T(2,128)(2,1)S(1)}, u32[]{:S(2)}, u32[]{:S(2)}) async-start(bf16[128,8,2,128]{3,2,0,1:T(2,128)(2,1)} %copy.92), calls=%async_computation.4 | async-start | bytes 1048576 | tf_op jit(solution)/shard_map/all_to_all | solution.py:90
  57.5 14.9 %copy-start.2 = (bf16[128,8,2,128]{3,2,0,1:T(2,128)(2,1)}, bf16[128,8,2,128]{3,2,0,1:T(2,128)(2,1)S(1)}, u32[]{:S(2)}) copy-start(bf16[128,8,2,128]{3,2,0,1:T(2,128)(2,1)S(1)} %all-to-all-done.4) | copy-start | bytes 1572868
  57.5 14.9 %all-to-all-start.5 = ((bf16[128,8,2,128]{3,2,0,1:T(2,128)(2,1)}), bf16[128,8,2,128]{3,2,0,1:T(2,128)(2,1)S(1)}, u32[]{:S(2)}, u32[]{:S(2)}) async-start(bf16[128,8,2,128]{3,2,0,1:T(2,128)(2,1)} %copy.93), calls=%async_computation.5 | async-start | bytes 1048576 | tf_op jit(solution)/shard_map/all_to_all | solution.py:91
  72.5 15.1 %copy-start.3 = (bf16[128,8,2,128]{3,2,0,1:T(2,128)(2,1)}, bf16[128,8,2,128]{3,2,0,1:T(2,128)(2,1)S(1)}, u32[]{:S(2)}) copy-start(bf16[128,8,2,128]{3,2,0,1:T(2,128)(2,1)S(1)} %all-to-all-done.5) | copy-start | bytes 1572868
  72.5 15.1 %all-to-all-start.3 = ((bf16[128,8,2,128]{3,2,0,1:T(2,128)(2,1)}), bf16[128,8,2,128]{3,2,0,1:T(2,128)(2,1)S(1)}, u32[]{:S(2)}, u32[]{:S(2)}) async-start(bf16[128,8,2,128]{3,2,0,1:T(2,128)(2,1)} %copy.91), calls=%async_computation.3 | async-start | bytes 1048576 | tf_op jit(solution)/shard_map/all_to_all | solution.py:89
  87.6 15.1 %all-to-all-start = ((bf16[128,8,2,128]{3,2,0,1:T(2,128)(2,1)}), bf16[128,8,2,128]{3,2,0,1:T(2,128)(2,1)S(1)}, u32[]{:S(2)}, u32[]{:S(2)}) async-start(bf16[128,8,2,128]{3,2,0,1:T(2,128)(2,1)} %copy.88), calls=%async_computation | async-start | bytes 1048576 | tf_op jit(solution)/shard_map/all_to_all | solution.py:86
  107.6 2.2 copy-start.13
  112.0 1.9 copy-start.8
  112.0 1.9 copy-start.9
  122.4 2.2 copy-start.13
  126.9 1.9 copy-start.8
  126.9 1.9 copy-start.9
  134.7 14.6 %all-to-all-start.6 = ((bf16[1024,1,2,128]{3,2,1,0:T(2,128)(2,1)}), bf16[1024,1,2,128]{3,2,1,0:T(2,128)(2,1)S(1)}, u32[]{:S(2)}, u32[]{:S(2)}) async-start(bf16[1024,1,2,128]{3,2,1,0:T(2,128)(2,1)} %copy.101), calls=%async_computation.6 | async-start | bytes 1048576 | tf_op jit(solution)/shard_map/all_to_all | solution.py:101
  149.3 15.3 %all-to-all-start.7 = ((bf16[1024,1,2,128]{3,2,1,0:T(2,128)(2,1)}), bf16[1024,1,2,128]{3,2,1,0:T(2,128)(2,1)S(1)}, u32[]{:S(2)}, u32[]{:S(2)}) async-start(bf16[1024,1,2,128]{3,2,1,0:T(2,128)(2,1)} %copy.107), calls=%async_computation.7 | async-start | bytes 1048576 | tf_op jit(solution)/shard_map/all_to_all | solution.py:102
  155.8 744.1 %all-gather.4.cloned.1.call-start = ((), (), s32[]{:S(2)}) async-start(), calls=%async_computation.9 | async-start | bytes 7077888 | tf_op jit(solution)/shard_map/all_gather | solution.py:123
  792.7 4.0 copy-start.7
  799.3 2.5 copy-start.6
  801.8 220.7 %reduce-scatter.2.cloned.1.call-start = ((), (), s32[]{:S(2)}) async-start(), calls=%async_computation.10 | async-start | bytes 3244032 | tf_op jit(solution)/shard_map/reduce_scatter | solution.py:127
  906.3 116.2 %copy-start.1 = (bf16[1,256,2048]{2,1,0:T(8,128)(2,1)S(1)}, bf16[1,256,2048]{2,1,0:T(8,128)(2,1)}, u32[]{:S(2)}) copy-start(bf16[1,256,2048]{2,1,0:T(8,128)(2,1)} %param.13) | copy-start | bytes 3145732
  (7 other events, 8.6 us)
Sparse Core Ops, SparseCore 0:
  9.9 730.0 all-gather.5
  801.9 97.9 all-gather.3
  906.4 116.0 reduce-scatter.1
where the time goes:
time: 1040 us; the launch traced here: 1030 us
  waiting for transfers between devices  813 us (78%)
  local copies, waits for them, and re-layouts  71.2 us (7%)
  matrix products  70.8 us (7%)
  starting transfers between devices  49.6 us (5%)
  between operations  14.6 us (1%)
    all_gather x1, waiting for transfers between devices, on_device(): full_weight = lax.all_gather(out_weight, ('dp', 'head'), axis=0, tiled=True)  575 us
    all_gather x1, waiting for transfers between devices, on_device(): clip_cotangent = lax.all_gather(cotangent, 'head', axis=0, tiled=True)  97.5 us
    reduce_scatter x1, waiting for transfers between devices, on_device(): lax.psum_scatter(lax.dot_general(clip_cotangent, attn_flat, (((0,), (0,))...  90.4 us
    dot_general x2, matrix products, project(): jnp.einsum('tgf,dgf->gtd', grouped, weight_groups, preferred_element_type...  23.9 us
    reshape x1, local copies, waits for them, and re-layouts, on_device(): weight_groups = full_weight.reshape(width, head_groups, group_width)  22.6 us
  transfers between devices with their start and end apart: 11, of which 11 were waited for; matrix products, arithmetic and copies ran while one was open for 7% of the time, Pallas kernels for 0%

commit v1 on v0

v1 whole, which is shorter than its diff:
```python
import math

import jax
import jax.numpy as jnp
from jax import lax
from jax.experimental import pallas as pl
from jax.experimental.pallas import tpu as pltpu
from jax.sharding import PartitionSpec as P

MESH = pl.DeviceIdType.MESH
HD = 128
GROUP = 256
TOK = 128
SRC_DEV = 256
MERGED = 1024
F = 2048
D = 3072
ROWS = 96
SCALE = 1.0 / math.sqrt(HD)

PEERS = ((0, 1), (1, 0), (1, 1), (3, 0), (3, 1), (2, 0), (2, 1))


def place():
    dp = lax.axis_index("dp")
    head = lax.axis_index("head")
    return dp // 16, (dp // 2) % 8, dp % 2, head // 4, head % 4


def dp_of(y_lo, z, core):
    return y_lo * 16 + z * 2 + core


def dot_t(a, b):
    return lax.dot_general(a, b, (((1,), (1,)), ((), ())), preferred_element_type=jnp.float32)


def front_kernel(
    q_hbm, k_hbm, tq_hbm, tk_hbm, v_hbm, tv_hbm, slot_ref, gap_ref, w_in,
    tok_ref, own_ref, w_out,
    stage, send, recv, send2, recv2, k2, v2, w_recv, w_own,
    in_sem, self_sem, a_send, a_recv, p_send, p_recv, w_send, w_rcv, w_self,
    y_send, y_recv, z_send, z_recv, s_send, s_recv,
):
    y_lo, z, core, y_hi, x = place()
    dp = lax.axis_index("dp")
    me = y_hi * 4 + x

    loads = []
    for i, ref in enumerate((q_hbm, k_hbm, tq_hbm, tk_hbm, v_hbm, tv_hbm)):
        load = pltpu.make_async_copy(ref, stage.at[i], in_sem.at[i])
        load.start()
        loads.append(load)

    def peer(r):
        dx, dy = PEERS[r]
        return ((y_hi + dy) % 2) * 4 + (x + dx) % 4

    peers = [peer(r) for r in range(7)]
    sibling = (dp_of(y_lo, z, 1 - core), me)
    partner = (dp_of(1 - y_lo, z, core), me)
    up = (dp_of(y_lo, (z + 1) % 8, core), me)
    down = (dp_of(y_lo, (z + 7) % 8, core), me)

    barrier = pltpu.get_barrier_semaphore()
    for p in peers:
        pl.semaphore_signal(barrier, inc=1, device_id=(dp, p), device_id_type=MESH)
    for who in (sibling, partner, up, down):
        pl.semaphore_signal(barrier, inc=1, device_id=who, device_id_type=MESH)
    pl.semaphore_wait(barrier, 11)

    def remote(src, dst, ssem, rsem, who):
        return pltpu.make_async_remote_copy(
            src_ref=src, dst_ref=dst, send_sem=ssem, recv_sem=rsem,
            device_id=who, device_id_type=MESH,
        )

    w_copies = []
    for r in range(7):
        copy = remote(w_in, w_recv.at[me], w_send.at[r], w_rcv.at[r], (dp, peers[r]))
        copy.start()
        w_copies.append(copy)
    w_local = pltpu.make_async_copy(w_in, w_recv.at[me], w_self.at[0])
    w_local.start()

    rows = lax.broadcasted_iota(jnp.int32, (TOK, SRC_DEV), 0)
    select = slot_ref[...] == rows
    counts = jnp.sum(select.astype(jnp.float32), axis=1, keepdims=True)
    inverse = 1.0 / counts
    onehot = select.astype(jnp.bfloat16)

    def merge(i):
        loads[i].wait()

        def body(h, carry):
            col = pl.multiple_of(h * GROUP, GROUP)
            total = jnp.dot(
                onehot, stage[i, :, pl.ds(col, GROUP)], preferred_element_type=jnp.float32
            )
            merged = (total * inverse).astype(jnp.bfloat16)
            send[h, 0, i] = merged[:, :HD]
            send[h, 1, i] = merged[:, HD:]
            return carry

        lax.fori_loop(0, 8, body, 0)

    def exchange(r, j, a):
        return remote(
            send.at[peers[r], j, pl.ds(3 * a, 3)],
            recv.at[j, me, pl.ds(3 * a, 3)],
            a_send.at[r, j, a],
            a_recv.at[r, j, a],
            (dp, peers[r]),
        )

    for i in range(3):
        merge(i)
    for r in range(7):
        exchange(r, 0, 0).start()
    for i in range(3, 6):
        merge(i)
    for j, a in ((0, 1), (1, 0), (1, 1)):
        for r in range(7):
            exchange(r, j, a).start()
    selfs = []
    for j in range(2):
        copy = pltpu.make_async_copy(send.at[me, j], recv.at[j, me], self_sem.at[j])
        copy.start()
        selfs.append(copy)

    for copy in w_copies:
        copy.wait()
    w_local.wait()
    out_row = lax.broadcasted_iota(jnp.int32, (ROWS, 128), 0)
    in_row = lax.broadcasted_iota(jnp.int32, (ROWS, 128), 1)
    pick = (in_row == (out_row // 12) * 16 + out_row % 12).astype(jnp.bfloat16)
    w_own[...] = jnp.dot(
        pick, w_recv[...].reshape(128, F), preferred_element_type=jnp.float32
    ).astype(jnp.bfloat16)

    def slot(b, plane):
        held = y_lo if b == 0 else 1 - y_lo
        return w_out.at[held * 8 + plane, core]

    pending = []

    def ring(way, step, b, src, plane):
        copy = remote(
            src, slot(b, plane), z_send.at[way, step, b], z_recv.at[way, step, b],
            up if way == 0 else down,
        )
        copy.start()
        pending.append(copy)

    def landed(way, step, b):
        plane = (z + (8 - step if way == 0 else step)) % 8
        ref = slot(b, plane)
        remote(
            ref, ref, z_send.at[way, step - 1, b], z_recv.at[way, step - 1, b],
            up if way == 0 else down,
        ).wait_recv()
        return ref, plane

    across = []

    def to_sibling(src, dst):
        n = len(across)
        copy = remote(src, dst, s_send.at[n], s_recv.at[n], sibling)
        copy.start()
        across.append(copy)

    own_slot = slot(0, z)
    ring(0, 0, 0, w_own, z)
    ring(1, 0, 0, w_own, z)
    to_partner = remote(w_own, own_slot, y_send.at[0], y_recv.at[0], partner)
    to_partner.start()
    to_sibling(w_own, own_slot)
    keep = pltpu.make_async_copy(w_own, own_slot, w_self.at[1])
    keep.start()
    other = slot(1, z)
    remote(other, other, y_send.at[0], y_recv.at[0], partner).wait_recv()
    ring(0, 0, 1, other, z)
    ring(1, 0, 1, other, z)
    to_sibling(other, other)

    def ring_step(step, b):
        for way in range(2):
            if step == 4 and way != b:
                continue
            ref, plane = landed(way, step, b)
            if step < 3 or (step == 3 and way == b):
                ring(way, step, b, ref, plane)
            to_sibling(ref, ref)

    gap = gap_ref[0, 0]

    def attend(j):
        for a in range(2):
            for r in range(7):
                exchange(r, j, a).wait_recv()
        selfs[j].wait()
        for t in range(8):
            here = pl.ds(t * TOK, TOK)
            k2[here, :HD] = recv[j, t, 1]
            k2[here, HD:] = recv[j, t, 3]
            v2[here, :HD] = recv[j, t, 4]
            v2[here, HD:] = recv[j, t, 5]

        def block(n, carry):
            q = recv[j, pl.ds(2 * n, 2), 0].reshape(2 * TOK, HD)
            tq = recv[j, pl.ds(2 * n, 2), 2].reshape(2 * TOK, HD)
            scores = dot_t(q, k2[:, :HD])
            scores_dot = dot_t(jnp.concatenate([tq, q], axis=1), k2[...])
            highest = jnp.max(scores, axis=1, keepdims=True)
            weights = jnp.exp((scores - highest) * SCALE)
            total = jnp.sum(weights, axis=1, keepdims=True)
            mean = jnp.sum(weights * scores_dot, axis=1, keepdims=True) / total
            tangent = (weights * (scores_dot - mean)).astype(jnp.bfloat16)
            mixed = jnp.dot(
                weights.astype(jnp.bfloat16), v2[...], preferred_element_type=jnp.float32
            )
            moved = jnp.dot(tangent, v2[:, :HD], preferred_element_type=jnp.float32)
            norm = 1.0 / total
            attn = mixed[:, :HD] * norm
            attn_dot = (moved * SCALE + mixed[:, HD:]) * norm
            both = (attn + gap * attn_dot).astype(jnp.bfloat16)
            start = pl.multiple_of(n * 2 * TOK, 2 * TOK)
            own_ref[pl.ds(start, 2 * TOK), j * HD : (j + 1) * HD] = attn.astype(jnp.bfloat16)
            send2[j, pl.ds(2 * n, 2)] = both.reshape(2, TOK, HD)
            return carry

        lax.fori_loop(0, 4, block, 0)

    def back(r, j):
        return remote(
            send2.at[j, peers[r]], recv2.at[j, me], p_send.at[r, j], p_recv.at[r, j],
            (dp, peers[r]),
        )

    ring_step(1, 0)
    ring_step(1, 1)
    attend(0)
    for r in range(7):
        back(r, 0).start()
    ring_step(2, 0)
    ring_step(2, 1)
    attend(1)
    for r in range(7):
        back(r, 1).start()
    recv2[:, pl.ds(me, 1)] = send2[:, pl.ds(me, 1)]
    ring_step(3, 0)
    for j in range(2):
        for r in range(7):
            back(r, j).wait_recv()
    for j in range(2):
        for h in range(8):
            col = h * GROUP + j * HD
            tok_ref[:, col : col + HD] = recv2[j, h]
    ring_step(3, 1)
    ring_step(4, 0)
    ring_step(4, 1)

    keep.wait()
    to_partner.wait_send()
    for copy in pending:
        copy.wait_send()
    for copy in across:
        copy.wait()
    for r in range(7):
        for j in range(2):
            back(r, j).wait_send()
            for a in range(2):
                exchange(r, j, a).wait_send()


def front(queries, key_states, queries_dot, keys_dot, value_states, values_dot, slot, gap, w_in):
    any_spec = pl.BlockSpec(memory_space=pl.ANY)
    vmem = pl.BlockSpec(memory_space=pltpu.VMEM)
    bf = jnp.bfloat16
    dma = pltpu.SemaphoreType.DMA
    return pl.pallas_call(
        front_kernel,
        out_shape=(
            jax.ShapeDtypeStruct((TOK, F), bf),
            jax.ShapeDtypeStruct((MERGED, GROUP), bf),
            jax.ShapeDtypeStruct((16, 2, ROWS, F), bf),
        ),
        in_specs=[any_spec] * 6 + [vmem, pl.BlockSpec(memory_space=pltpu.SMEM), vmem],
        out_specs=(vmem, vmem, any_spec),
        scratch_shapes=[
            pltpu.VMEM((6, SRC_DEV, F), bf),
            pltpu.VMEM((8, 2, 6, TOK, HD), bf),
            pltpu.VMEM((2, 8, 6, TOK, HD), bf),
            pltpu.VMEM((2, 8, TOK, HD), bf),
            pltpu.VMEM((2, 8, TOK, HD), bf),
            pltpu.VMEM((MERGED, 2 * HD), bf),
            pltpu.VMEM((MERGED, 2 * HD), bf),
            pltpu.VMEM((8, 16, F), bf),
            pltpu.VMEM((ROWS, F), bf),
            dma((6,)),
            dma((2,)),
            dma((7, 2, 2)),
            dma((7, 2, 2)),
            dma((7, 2)),
            dma((7, 2)),
            dma((7,)),
            dma((7,)),
            dma((2,)),
            dma((1,)),
            dma((1,)),
            dma((2, 4, 2)),
            dma((2, 4, 2)),
            dma((16,)),
            dma((16,)),
        ],
        compiler_params=pltpu.CompilerParams(
            collective_id=0, has_side_effects=True, vmem_limit_bytes=44 << 20
        ),
        cost_estimate=pl.CostEstimate(
            flops=5_000_000_000, bytes_accessed=32 << 20, transcendentals=2 << 20
        ),
    )(queries, key_states, queries_dot, keys_dot, value_states, values_dot, slot, gap, w_in)


def on_device(
    queries, key_states, value_states, queries_dot, keys_dot, values_dot,
    velocity, time_gap, merge_slot, out_weight,
):
    select = merge_slot[0][None, :] == jnp.arange(TOK, dtype=jnp.int32)[:, None]
    onehot = select.astype(jnp.bfloat16)
    counts = jnp.sum(select.astype(jnp.float32), axis=1)
    moved = jnp.dot(onehot, velocity[0], preferred_element_type=jnp.float32)
    attn_tok, attn_own, weights = front(
        queries[0], key_states[0], queries_dot[0], keys_dot[0], value_states[0], values_dot[0],
        merge_slot, time_gap.reshape(1, 1), jnp.pad(out_weight, ((0, 4), (0, 0))),
    )
    full_weight = weights.reshape(D, F)
    proj = dot_t(attn_tok, full_weight)
    cotangent = (counts[:, None] * proj - moved).astype(jnp.bfloat16)
    head_weight = lax.dynamic_slice_in_dim(
        full_weight, lax.axis_index("head") * GROUP, GROUP, 1
    )
    clip_cotangent = lax.all_gather(cotangent, "head", axis=0, tiled=True)
    grad_attn = jnp.dot(
        clip_cotangent, head_weight, preferred_element_type=jnp.float32
    ).astype(jnp.bfloat16)
    grad_weight = lax.psum_scatter(
        lax.dot_general(
            clip_cotangent, attn_own, (((0,), (0,)), ((), ())), preferred_element_type=jnp.float32
        ),
        "dp",
        scatter_dimension=0,
        tiled=True,
    )
    return (grad_attn[None], grad_weight)


def solution(mesh):
    block = P("dp", "head", None)
    return jax.shard_map(
        on_device,
        mesh=mesh,
        in_specs=(block,) * 7 + (P("dp"), P("dp", "head"), P(("dp", "head"), None)),
        out_specs=(P("dp", None, "head"), P("dp", "head")),
        check_vma=False,
    )
```

time: 1040 us -> 368 us (0.35)
  waiting for transfers between devices: 813 us -> 201 us
  Pallas kernels: 0 us -> 116 us
  local copies, waits for them, and re-layouts: 71.2 us -> 8.89 us
  starting transfers between devices: 49.6 us -> 0.08 us
  matrix products: 70.8 us -> 22.2 us
    all_gather x1 -> x0, waiting for transfers between devices: 575 us -> none  [on_device(): full_weight = lax.all_gather(out_weight, ('dp', 'head'), axis=0, tiled=True)]
    pallas_call x0 -> x1, Pallas kernels: none -> 116 us  [front(): pl.pallas_call(front_kernel, out_shape=(jax.ShapeDtypeStruct((TOK, F), bf...]
    all_to_all x8 -> x0, starting transfers between devices: 49.5 us -> none  [the longest x1 7 us: on_device(): lax.all_to_all(merged_k, 'head', split_axis=1, concat_axis=0, tiled=True)]
    all_to_all x8 -> x0, waiting for transfers between devices: 49.1 us -> none  [the longest x1 7.69 us: on_device(): lax.all_to_all(attn_heads_dot, 'head', split_axis=0, concat_axis=1, tiled...]
    dot_general x22 -> x3, matrix products: 58.4 us -> 16.4 us  [the longest x1 8.84 us: dot_t(): lax.dot_general(a, b, (((1,), (1,)), ((), ())), preferred_element_type=jn...]
    reshape x13 -> x0, local copies, waits for them, and re-layouts: 32.1 us -> none  [the longest x1 22.6 us: on_device(): weight_groups = full_weight.reshape(width, head_groups, group_width)]
    reduce_scatter x1, waiting for transfers between devices: 90.4 us -> 110 us  [on_device(): lax.psum_scatter(lax.dot_general(clip_cotangent, attn_own, (((0,), (0,)),...]
    while x30 -> x0, local copies, waits for them, and re-layouts: 12.6 us -> none  [the longest x6 6.38 us: attend(): outputs = lax.map(one_block, jnp.arange(length // block, dtype=jnp.int32))]
  transfers between devices with their start and end apart: 11 -> 2, of which waited for: 11 -> 2; matrix products, arithmetic and copies ran while one was open for 7% -> 2% of each run, Pallas kernels for 0% -> 0%
where the time goes in v1:
time: 368 us; the launch traced here: 363 us
  waiting for transfers between devices  201 us (55%)
  Pallas kernels  116 us (32%)
  matrix products  22.2 us (6%)
  between operations  14.8 us (4%)
  local copies, waits for them, and re-layouts  8.89 us (2%)
    pallas_call x1, Pallas kernels, front(): pl.pallas_call(front_kernel, out_shape=(jax.ShapeDtypeStruct((TOK, F), bf...  116 us
    reduce_scatter x1, waiting for transfers between devices, on_device(): lax.psum_scatter(lax.dot_general(clip_cotangent, attn_own, (((0,), (0,)),...  110 us
    all_gather x1, waiting for transfers between devices, on_device(): clip_cotangent = lax.all_gather(cotangent, 'head', axis=0, tiled=True)  90.5 us
    dot_general x1, matrix products, dot_t(): lax.dot_general(a, b, (((1,), (1,)), ((), ())), preferred_element_type=jn...  8.84 us
    unnamed x16, local copies, waits for them, and re-layouts  8.03 us
  transfers between devices with their start and end apart: 2, of which 2 were waited for; matrix products, arithmetic and copies ran while one was open for 2% of the time, Pallas kernels for 0%

profile of v1, /device:TPU:5, one launch (start us, length us, event | category | flops | bytes accessed | tf_op | source)
XLA Modules:
  0.0 363.5 jit_solution(16698284719486919132)
XLA Ops:
  7.2 0.0 copy-start
  7.2 0.0 all-gather.2.cloned.1.call-start
  8.0 0.8 convert_reduce_fusion
  8.8 0.9 pad.4.w_in
  9.6 0.0 copy-start.1
  9.6 0.7 copy-done.1
  10.3 0.0 copy-start.2
  10.3 1.2 copy-done.2
  11.5 1.2 copy-done.3
  12.8 1.2 copy-done.4
  14.0 1.2 copy-done.5
  15.2 1.2 copy-done.6
  16.4 1.2 copy-done.7
  17.7 115.8 %shard_map.113 = (bf16[128,2048]{1,0:T(8,128)(2,1)S(1)}, bf16[1024,256]{1,0:T(8,128)(2,1)S(1)}, bf16[16,2,96,2048]{3,2,1,0:T(8,128)(2,1)}) custom-call(bf16[256,2048]{1,0:T(8,128)(2,1)S(1)} %bitcast.22, bf16[256,2048]{1,0:T(8,128)(2,1)S(1)} %bitcast.23, bf16[256,2048]{1,0:T(8,128)(2,1)S(1)} %bitcast.24, bf16[256,2048]{1,0:T(8,128)(2,1)S(1)} %bitcast.25, ...), custom_call_target="tpu_custom_call" | custom-call | flops 5000000000 | bytes 33554432 | tf_op jit(solution)/shard_map/pallas_call | solution.py:281
  133.4 8.8 %convolution_multiply_fusion = f32[128,3072]{1,0:T(8,128)S(1)} fusion(bf16[128,2048]{1,0:T(8,128)(2,1)S(1)} %get-tuple-element.5, bf16[3072,2048]{1,0:T(8,128)(2,1)} %bitcast.28, f32[128]{0:T(128)S(1)} %convert_reduce_fusion), kind=kOutput, calls=%fused_computation.1 | convolution fusion | flops 1611005952 | bytes 14680576 | tf_op jit(solution)/shard_map/dot_general | solution.py:35
  142.3 0.0 copy-done
  142.3 1.3 fusion
  143.6 0.0 all-gather.2.cloned.1.call-update
  143.6 0.0 reduce-scatter.2.cloned.1.call-start
  143.7 90.5 %all-gather.2.cloned.1.call-done = bf16[1024,3072]{1,0:T(8,128)(2,1)} async-done(((bf16[128,3072]{1,0:T(8,128)(2,1)}), bf16[1024,3072]{1,0:T(8,128)(2,1)}) %all-gather.2.cloned.1.call-update) | async-done | bytes 6291472 | tf_op jit(solution)/shard_map/all_gather | solution.py:343
  234.1 6.3 %fusion.12 = f32[3072,256]{1,0:T(8,128)} fusion(bf16[1024,3072]{1,0:T(8,128)(2,1)} %all-gather.2.cloned.1.call-done, bf16[1024,256]{1,0:T(8,128)(2,1)S(1)} %get-tuple-element.7), kind=kOutput, calls=%fused_computation.12 | convolution fusion | flops 1610612736 | bytes 9961472 | tf_op jit(solution)/shard_map/dot_general | solution.py:348
  240.4 0.0 reduce-scatter.2.cloned.1.call-update
  240.5 5.8 %fusion.7 = bf16[1,1024,256]{2,1,0:T(8,128)(2,1)} fusion(bf16[1024,3072]{1,0:T(8,128)(2,1)} %all-gather.2.cloned.1.call-done, bf16[3072,2048]{1,0:T(8,128)(2,1)} %bitcast.29, s32[]{:T(128)S(6)} %select_n.3), kind=kOutput, calls=%fused_computation.7 | convolution fusion | flops 1610874880 | bytes 8388612 | tf_op jit(solution)/shard_map/dot_general | solution.py:344
  246.3 110.4 %reduce-scatter.2.cloned.1.call-done = f32[96,256]{1,0:T(8,128)} async-done(((f32[3072,256]{1,0:T(8,128)}), f32[96,256]{1,0:T(8,128)}) %reduce-scatter.2.cloned.1.call-update) | async-done | bytes 98320 | tf_op jit(solution)/shard_map/reduce_scatter | solution.py:347
  (5 shorter events, 0.0 us)
Async XLA Ops:
  7.2 135.1 %copy-start = (bf16[1,256,3072]{2,1,0:T(8,128)(2,1)S(1)}, bf16[1,256,3072]{2,1,0:T(8,128)(2,1)}, u32[]{:S(2)}) copy-start(bf16[1,256,3072]{2,1,0:T(8,128)(2,1)} %param.16) | copy-start | bytes 4718596
  7.2 226.9 %all-gather.2.cloned.1.call-start = ((), (), s32[]{:S(2)}) async-start(), calls=%async_computation.1 | async-start | bytes 7077888 | tf_op jit(solution)/shard_map/all_gather | solution.py:343
  9.6 0.7 copy-start.1
  10.3 1.2 copy-start.2
  11.5 1.2 copy-start.3
  12.8 1.2 copy-start.4
  14.0 1.2 copy-start.5
  15.2 1.2 copy-start.6
  16.4 1.2 copy-start.7
  143.6 213.0 %reduce-scatter.2.cloned.1.call-start = ((), (), s32[]{:S(2)}) async-start(), calls=%async_computation.2 | async-start | bytes 3244032 | tf_op jit(solution)/shard_map/reduce_scatter | solution.py:347
Sparse Core Ops, SparseCore 0:
  143.7 90.3 all-gather.1
  240.6 116.0 reduce-scatter.1

commit v2 on v1

v2 whole, which is shorter than its diff:
```python
import math

import jax
import jax.numpy as jnp
from jax import lax
from jax.experimental import pallas as pl
from jax.experimental.pallas import tpu as pltpu
from jax.sharding import PartitionSpec as P

MESH = pl.DeviceIdType.MESH
HD = 128
GROUP = 256
TOK = 128
SRC_DEV = 256
MERGED = 1024
F = 2048
D = 3072
ROWS = 96
SCALE = 1.0 / math.sqrt(HD)

PEERS = ((0, 1), (1, 0), (1, 1), (3, 0), (3, 1), (2, 0), (2, 1))


def place():
    dp = lax.axis_index("dp")
    head = lax.axis_index("head")
    return dp // 16, (dp // 2) % 8, dp % 2, head // 4, head % 4


def dp_of(y_lo, z, core):
    return y_lo * 16 + z * 2 + core


def dot_t(a, b):
    return lax.dot_general(a, b, (((1,), (1,)), ((), ())), preferred_element_type=jnp.float32)


def clip_kernel(
    q_hbm, k_hbm, tq_hbm, tk_hbm, v_hbm, tv_hbm, vel_hbm, slot_ref, gap_ref, w_in,
    ga_ref, gw_ref,
    stage, vel, send, recv, send2, own, k2, v2, w_recv, w_own, w_all, tok, full, acc,
    c_send_buf, quarter, g_buf, term, term_sib, rs_buf, rs_recv, fin,
    in_sem, self_sem, a_send, a_recv, p_send, p_recv, f_send, f_recv, w_send, w_rcv, w_self,
    y_send, y_recv, z_send, z_recv, s_send, s_recv, c_send, c_recv, g_send, g_recv,
    b_send, b_recv, r_send, r_recv, e_send, e_recv,
):
    y_lo, z, core, y_hi, x = place()
    dp = lax.axis_index("dp")
    me = y_hi * 4 + x

    loads = []
    for i, ref in enumerate((q_hbm, k_hbm, tq_hbm, tk_hbm, v_hbm, tv_hbm)):
        load = pltpu.make_async_copy(ref, stage.at[i], in_sem.at[i])
        load.start()
        loads.append(load)
    vel_load = pltpu.make_async_copy(vel_hbm, vel, in_sem.at[6])
    vel_load.start()

    peers = [((y_hi + dy) % 2) * 4 + (x + dx) % 4 for dx, dy in PEERS]
    sibling = (dp_of(y_lo, z, 1 - core), me)
    partner = (dp_of(1 - y_lo, z, core), me)
    up = (dp_of(y_lo, (z + 1) % 8, core), me)
    down = (dp_of(y_lo, (z + 7) % 8, core), me)

    turn = (z + 7) % 8
    dest_x = turn % 4
    dest_z = 4 * (x % 2) + 2 * ((y_lo + dest_x + 1) % 2) + turn // 4
    dest = (dp_of(x // 2, dest_z, core), y_hi * 4 + dest_x)
    from_x = 2 * y_lo + z // 4
    from_z = (((z % 4) % 2) * 4 + x + 1) % 8
    source = (dp_of(((z % 4) // 2 + x + 1) % 2, from_z, core), y_hi * 4 + from_x)

    barrier = pltpu.get_barrier_semaphore()

    def greet(who):
        pl.semaphore_signal(barrier, inc=1, device_id=who, device_id_type=MESH)

    for p in peers:
        greet((dp, p))
    for dy in range(2):
        for dz in range(8):
            if dy or dz:
                greet((dp_of((y_lo + dy) % 2, (z + dz) % 8, core), me))
    greet(sibling)
    greet(dest)
    greet(source)
    pl.semaphore_wait(barrier, 25)

    def remote(src, dst, ssem, rsem, who):
        return pltpu.make_async_remote_copy(
            src_ref=src, dst_ref=dst, send_sem=ssem, recv_sem=rsem,
            device_id=who, device_id_type=MESH,
        )

    w_copies = []
    for r in range(7):
        copy = remote(w_in, w_recv.at[me], w_send.at[r], w_rcv.at[r], (dp, peers[r]))
        copy.start()
        w_copies.append(copy)
    w_local = pltpu.make_async_copy(w_in, w_recv.at[me], w_self.at[0])
    w_local.start()

    rows = lax.broadcasted_iota(jnp.int32, (TOK, SRC_DEV), 0)
    select = slot_ref[...] == rows
    counts = jnp.sum(select.astype(jnp.float32), axis=1, keepdims=True)
    inverse = 1.0 / counts
    onehot = select.astype(jnp.bfloat16)

    def merge(i):
        loads[i].wait()

        def body(h, carry):
            col = pl.multiple_of(h * GROUP, GROUP)
            total = jnp.dot(
                onehot, stage[i, :, pl.ds(col, GROUP)], preferred_element_type=jnp.float32
            )
            merged = (total * inverse).astype(jnp.bfloat16)
            send[h, 0, i] = merged[:, :HD]
            send[h, 1, i] = merged[:, HD:]
            return carry

        lax.fori_loop(0, 8, body, 0)

    def exchange(r, j, a):
        return remote(
            send.at[peers[r], j, pl.ds(3 * a, 3)],
            recv.at[j, me, pl.ds(3 * a, 3)],
            a_send.at[r, j, a],
            a_recv.at[r, j, a],
            (dp, peers[r]),
        )

    for i in range(3):
        merge(i)

    for copy in w_copies:
        copy.wait()
    w_local.wait()
    out_row = lax.broadcasted_iota(jnp.int32, (ROWS, 128), 0)
    in_row = lax.broadcasted_iota(jnp.int32, (ROWS, 128), 1)
    pick = (in_row == (out_row // 12) * 16 + out_row % 12).astype(jnp.bfloat16)
    w_own[...] = jnp.dot(
        pick, w_recv[...].reshape(128, F), preferred_element_type=jnp.float32
    ).astype(jnp.bfloat16)

    def slot(b, plane):
        held = y_lo if b == 0 else 1 - y_lo
        first = pl.multiple_of(dp_of(held, plane, core) * ROWS, ROWS)
        return w_all.at[pl.ds(first, ROWS)]

    pending = []

    def ring(way, step, b, src, plane):
        copy = remote(
            src, slot(b, plane), z_send.at[way, step, b], z_recv.at[way, step, b],
            up if way == 0 else down,
        )
        copy.start()
        pending.append(copy)

    def landed(way, step, b):
        plane = (z + (8 - step if way == 0 else step)) % 8
        ref = slot(b, plane)
        remote(
            ref, ref, z_send.at[way, step - 1, b], z_recv.at[way, step - 1, b],
            up if way == 0 else down,
        ).wait_recv()
        return ref, plane

    across = []

    def to_sibling(src, dst):
        n = len(across)
        copy = remote(src, dst, s_send.at[n], s_recv.at[n], sibling)
        copy.start()
        across.append(copy)

    taken = [0]

    def from_sibling(upto):
        for n in range(taken[0], upto):
            across[n].wait_recv()
        taken[0] = upto

    own_slot = slot(0, z)
    to_partner = remote(w_own, own_slot, y_send.at[0], y_recv.at[0], partner)
    to_partner.start()
    ring(0, 0, 0, w_own, z)
    ring(1, 0, 0, w_own, z)
    to_sibling(w_own, own_slot)
    keep = pltpu.make_async_copy(w_own, own_slot, w_self.at[1])
    keep.start()

    for r in range(7):
        exchange(r, 0, 0).start()
    for i in range(3, 6):
        merge(i)
    for j, a in ((0, 1), (1, 0), (1, 1)):
        for r in range(7):
            exchange(r, j, a).start()
    selfs = []
    for j in range(2):
        copy = pltpu.make_async_copy(send.at[me, j], recv.at[j, me], self_sem.at[j])
        copy.start()
        selfs.append(copy)

    other = slot(1, z)
    remote(other, other, y_send.at[0], y_recv.at[0], partner).wait_recv()
    ring(0, 0, 1, other, z)
    ring(1, 0, 1, other, z)
    to_sibling(other, other)

    def ring_step(step, b):
        for way in range(2):
            if step == 4 and way != b:
                continue
            ref, plane = landed(way, step, b)
            if step < 3 or (step == 3 and way == b):
                ring(way, step, b, ref, plane)
            to_sibling(ref, ref)

    gap = gap_ref[0, 0]

    def attend(j):
        for a in range(2):
            for r in range(7):
                exchange(r, j, a).wait_recv()
        selfs[j].wait()
        for t in range(8):
            here = pl.ds(t * TOK, TOK)
            k2[here, :HD] = recv[j, t, 1]
            k2[here, HD:] = recv[j, t, 3]
            v2[here, :HD] = recv[j, t, 4]
            v2[here, HD:] = recv[j, t, 5]

        def block(n, carry):
            q = recv[j, pl.ds(2 * n, 2), 0].reshape(2 * TOK, HD)
            tq = recv[j, pl.ds(2 * n, 2), 2].reshape(2 * TOK, HD)
            scores = dot_t(q, k2[:, :HD])
            scores_dot = dot_t(jnp.concatenate([tq, q], axis=1), k2[...])
            highest = jnp.max(scores, axis=1, keepdims=True)
            weights = jnp.exp((scores - highest) * SCALE)
            total = jnp.sum(weights, axis=1, keepdims=True)
            mean = jnp.sum(weights * scores_dot, axis=1, keepdims=True) / total
            tangent = (weights * (scores_dot - mean)).astype(jnp.bfloat16)
            mixed = jnp.dot(
                weights.astype(jnp.bfloat16), v2[...], preferred_element_type=jnp.float32
            )
            moved = jnp.dot(tangent, v2[:, :HD], preferred_element_type=jnp.float32)
            norm = 1.0 / total
            attn = mixed[:, :HD] * norm
            attn_dot = (moved * SCALE + mixed[:, HD:]) * norm
            both = (attn + gap * attn_dot).astype(jnp.bfloat16)
            start = pl.multiple_of(n * 2 * TOK, 2 * TOK)
            own[j, pl.ds(start, 2 * TOK)] = attn.astype(jnp.bfloat16)
            send2[j, pl.ds(2 * n, 2)] = both.reshape(2, TOK, HD)
            return carry

        lax.fori_loop(0, 4, block, 0)

    def back(r, j):
        col = pl.multiple_of(me * GROUP + j * HD, HD)
        return remote(
            send2.at[j, peers[r]], tok.at[:, pl.ds(col, HD)], p_send.at[r, j], p_recv.at[r, j],
            (dp, peers[r]),
        )

    def along(dx, j):
        col = pl.multiple_of(x * GROUP + j * HD, HD)
        return remote(
            own.at[j], full.at[:, pl.ds(col, HD)], f_send.at[dx - 1, j], f_recv.at[dx - 1, j],
            (dp, y_hi * 4 + (x + dx) % 4),
        )

    locals_ = []

    def hand_out(j):
        for r in range(7):
            back(r, j).start()
        for dx in (1, 3, 2):
            along(dx, j).start()
        col = pl.multiple_of(me * GROUP + j * HD, HD)
        copy = pltpu.make_async_copy(send2.at[j, me], tok.at[:, pl.ds(col, HD)], self_sem.at[2 + j])
        copy.start()
        locals_.append(copy)
        col = pl.multiple_of(x * GROUP + j * HD, HD)
        copy = pltpu.make_async_copy(own.at[j], full.at[:, pl.ds(col, HD)], self_sem.at[4 + j])
        copy.start()
        locals_.append(copy)

    ring_step(1, 0)
    ring_step(1, 1)
    attend(0)
    hand_out(0)
    ring_step(2, 0)
    ring_step(2, 1)
    attend(1)
    hand_out(1)
    vel_load.wait()
    for j in range(2):
        for r in range(7):
            back(r, j).wait_recv()
    for copy in locals_:
        copy.wait()
    keep.wait()

    near = z // 2
    side = 1 - 2 * (z % 2)
    pairs = (near, (near + 4 - side) % 4, (near + side) % 4, (near + 2) % 4)

    def quarter_copy(n, lo, way):
        pair = pairs[n]
        to = 2 * lo + pair // 2
        half = pair % 2
        col = pl.multiple_of(me * TOK, TOK)
        y_to = (y_hi + way) % 2
        return remote(
            c_send_buf.at[n, lo], quarter.at[half, :, pl.ds(col, TOK)],
            c_send.at[n, lo, way], c_recv.at[half, way * 4 + (to + 4 - x) % 4],
            (dp, y_to * 4 + to),
        )

    def local_quarter(n, lo):
        half = pairs[n] % 2
        col = pl.multiple_of(me * TOK, TOK)
        return pltpu.make_async_copy(
            c_send_buf.at[n, lo], quarter.at[half, :, pl.ds(col, TOK)], self_sem.at[6 + half]
        )

    def project(n):
        pair = pairs[n]
        for lo in range(2):
            first = pl.multiple_of(lo * 1536 + pair * 384, 384)
            weights = w_all[pl.ds(first, 384)]
            proj = dot_t(tok[...], weights)
            moved = jnp.dot(
                onehot, vel[:, pl.ds(first, 384)], preferred_element_type=jnp.float32
            )
            cot = counts * proj - moved
            c_send_buf[n, lo] = cot.T.astype(jnp.bfloat16)
            to = 2 * lo + pair // 2
            quarter_copy(n, lo, 1).start()

            @pl.when(to != x)
            def _():
                quarter_copy(n, lo, 0).start()

            @pl.when(to == x)
            def _():
                local_quarter(n, lo).start()

            part = jnp.dot(cot.astype(jnp.bfloat16), weights, preferred_element_type=jnp.float32)
            if n == 0 and lo == 0:
                acc[...] = part
            else:
                acc[...] += part

    from_sibling(6)
    project(0)
    from_sibling(10)
    project(1)
    ring_step(3, 0)
    ring_step(3, 1)
    from_sibling(14)
    project(2)
    ring_step(4, 0)
    ring_step(4, 1)
    from_sibling(16)
    project(3)

    def grads(r):
        here = pl.ds(pl.multiple_of(me * TOK, TOK), TOK)
        return remote(
            g_buf.at[peers[r]], ga_ref.at[here], g_send.at[r], g_recv.at[r], (dp, peers[r])
        )

    for h in range(8):
        g_buf[h] = acc[:, h * GROUP : (h + 1) * GROUP].astype(jnp.bfloat16)
    for r in range(7):
        grads(r).start()
    ga_own = pltpu.make_async_copy(
        g_buf.at[me], ga_ref.at[pl.ds(pl.multiple_of(me * TOK, TOK), TOK)], self_sem.at[8]
    )
    ga_own.start()

    early = (near % 2 + (near // 2 + x) % 2) % 2
    halves = (early, 1 - early)

    def half_term(half):
        for way in range(2):
            for dx in range(4):
                if way or dx:
                    col = pl.multiple_of(me * TOK, TOK)
                    remote(
                        c_send_buf.at[0, 0], quarter.at[half, :, pl.ds(col, TOK)],
                        c_send.at[0, 0, 0], c_recv.at[half, way * 4 + dx], sibling,
                    ).wait_recv()
        pltpu.make_async_copy(
            c_send_buf.at[0, 0], quarter.at[half, :, pl.ds(0, TOK)], self_sem.at[6 + half]
        ).wait()
        for block in range(4):
            part = jnp.dot(
                quarter[half], full[:, block * GROUP : (block + 1) * GROUP],
                preferred_element_type=jnp.float32,
            )
            for zi in range(2):
                for c in range(2):
                    top = zi * 192 + c * ROWS
                    term[half, c, zi, block] = part[top : top + ROWS]
        copy = swap(half)
        copy.start()

    def swap(half):
        return remote(
            term.at[half, 1 - core], term_sib.at[half], b_send.at[half], b_recv.at[half], sibling
        )

    def reduce_copy(half, dz):
        turn_to = (z + dz + 7) % 8
        zi = turn_to // 4
        block = turn_to % 4
        lo = (half + block + 1) % 2
        rel = ((lo + y_lo) % 2) * 8 + dz
        return lo, zi, block, remote(
            rs_buf.at[half, zi, block], rs_recv.at[rel], r_send.at[half, dz], r_recv.at[rel],
            (dp_of(lo, (z + dz) % 8, core), me),
        )

    def spread(half):
        swap(half).wait_recv()
        for dz in (4, 3, 5, 2, 6, 1, 7, 0):
            lo, zi, block, copy = reduce_copy(half, dz)
            rs_buf[half, zi, block] = (
                term[half, core, zi, block] + term_sib[half, zi, block]
            ).astype(jnp.bfloat16)
            if dz:
                copy.start()
            else:

                @pl.when(lo != y_lo)
                def _():
                    copy.start()

                @pl.when(lo == y_lo)
                def _():
                    rs_recv[0] = rs_buf[half, zi, block]

    for dx in (1, 3, 2):
        for j in range(2):
            along(dx, j).wait_recv()
    for half in halves:
        half_term(half)
    for half in halves:
        spread(half)

    for rel in range(1, 16):
        remote(
            rs_buf.at[0, 0, 0], rs_recv.at[rel], r_send.at[0, 0], r_recv.at[rel], sibling
        ).wait_recv()

    def add(rel, total):
        return total + rs_recv[rel].astype(jnp.float32)

    fin[...] = lax.fori_loop(0, 16, add, jnp.zeros((ROWS, GROUP), jnp.float32))
    place_copy = remote(fin, gw_ref, e_send.at[0], e_recv.at[0], dest)
    place_copy.start()

    to_partner.wait_send()
    for copy in pending:
        copy.wait_send()
    for copy in across:
        copy.wait_send()
    for r in range(7):
        for j in range(2):
            back(r, j).wait_send()
            for a in range(2):
                exchange(r, j, a).wait_send()
        grads(r).wait()
    ga_own.wait()
    for dx in (1, 3, 2):
        for j in range(2):
            along(dx, j).wait_send()
    for n in range(4):
        for lo in range(2):
            quarter_copy(n, lo, 1).wait_send()

            @pl.when(2 * lo + pairs[n] // 2 != x)
            def _():
                quarter_copy(n, lo, 0).wait_send()

    for half in range(2):
        swap(half).wait_send()
        for dz in range(8):
            lo, _, _, copy = reduce_copy(half, dz)
            if dz:
                copy.wait_send()
            else:

                @pl.when(lo != y_lo)
                def _():
                    copy.wait_send()

    place_copy.wait()


def clip_call(queries, key_states, queries_dot, keys_dot, value_states, values_dot, velocity, slot, gap, w_in):
    any_spec = pl.BlockSpec(memory_space=pl.ANY)
    vmem = pl.BlockSpec(memory_space=pltpu.VMEM)
    bf = jnp.bfloat16
    f32 = jnp.float32
    dma = pltpu.SemaphoreType.DMA
    return pl.pallas_call(
        clip_kernel,
        out_shape=(
            jax.ShapeDtypeStruct((MERGED, GROUP), bf),
            jax.ShapeDtypeStruct((ROWS, GROUP), f32),
        ),
        in_specs=[any_spec] * 7 + [vmem, pl.BlockSpec(memory_space=pltpu.SMEM), vmem],
        out_specs=(vmem, vmem),
        scratch_shapes=[
            pltpu.VMEM((6, SRC_DEV, F), bf),
            pltpu.VMEM((SRC_DEV, D), bf),
            pltpu.VMEM((8, 2, 6, TOK, HD), bf),
            pltpu.VMEM((2, 8, 6, TOK, HD), bf),
            pltpu.VMEM((2, 8, TOK, HD), bf),
            pltpu.VMEM((2, MERGED, HD), bf),
            pltpu.VMEM((MERGED, 2 * HD), bf),
            pltpu.VMEM((MERGED, 2 * HD), bf),
            pltpu.VMEM((8, 16, F), bf),
            pltpu.VMEM((ROWS, F), bf),
            pltpu.VMEM((D, F), bf),
            pltpu.VMEM((TOK, F), bf),
            pltpu.VMEM((MERGED, 4 * GROUP), bf),
            pltpu.VMEM((TOK, F), f32),
            pltpu.VMEM((4, 2, 384, TOK), bf),
            pltpu.VMEM((2, 384, MERGED), bf),
            pltpu.VMEM((8, TOK, GROUP), bf),
            pltpu.VMEM((2, 2, 2, 4, ROWS, GROUP), f32),
            pltpu.VMEM((2, 2, 4, ROWS, GROUP), f32),
            pltpu.VMEM((2, 2, 4, ROWS, GROUP), bf),
            pltpu.VMEM((16, ROWS, GROUP), bf),
            pltpu.VMEM((ROWS, GROUP), f32),
            dma((7,)),
            dma((9,)),
            dma((7, 2, 2)),
            dma((7, 2, 2)),
            dma((7, 2)),
            dma((7, 2)),
            dma((3, 2)),
            dma((3, 2)),
            dma((7,)),
            dma((7,)),
            dma((2,)),
            dma((1,)),
            dma((1,)),
            dma((2, 4, 2)),
            dma((2, 4, 2)),
            dma((16,)),
            dma((16,)),
            dma((4, 2, 2)),
            dma((2, 8)),
            dma((7,)),
            dma((7,)),
            dma((2,)),
            dma((2,)),
            dma((2, 8)),
            dma((16,)),
            dma((1,)),
            dma((1,)),
        ],
        compiler_params=pltpu.CompilerParams(
            collective_id=0, has_side_effects=True, vmem_limit_bytes=60 << 20
        ),
        cost_estimate=pl.CostEstimate(
            flops=10_000_000_000, bytes_accessed=9 << 20, transcendentals=2 << 20
        ),
    )(
        queries, key_states, queries_dot, keys_dot, value_states, values_dot, velocity,
        slot, gap, w_in,
    )


def on_device(
    queries, key_states, value_states, queries_dot, keys_dot, values_dot,
    velocity, time_gap, merge_slot, out_weight,
):
    grad_attn, grad_weight = clip_call(
        queries[0], key_states[0], queries_dot[0], keys_dot[0], value_states[0], values_dot[0],
        velocity[0], merge_slot, time_gap.reshape(1, 1), jnp.pad(out_weight, ((0, 4), (0, 0))),
    )
    return (grad_attn[None], grad_weight)


def solution(mesh):
    block = P("dp", "head", None)
    return jax.shard_map(
        on_device,
        mesh=mesh,
        in_specs=(block,) * 7 + (P("dp"), P("dp", "head"), P(("dp", "head"), None)),
        out_specs=(P("dp", None, "head"), P("dp", "head")),
        check_vma=False,
    )
```

time: 368 us -> 162 us (0.44); the launches traced: 363 us -> 162 us
  waiting for transfers between devices: 201 us -> 0 us
  Pallas kernels: 116 us -> 156 us
  matrix products: 22.2 us -> 0 us
  between operations: 14.8 us -> 1.29 us
  local copies, waits for them, and re-layouts: 8.89 us -> 4.89 us
    reduce_scatter x1 -> x0, waiting for transfers between devices: 110 us -> none  [on_device(): lax.psum_scatter(lax.dot_general(clip_cotangent, attn_own, (((0,), (0,)),...]
    all_gather x1 -> x0, waiting for transfers between devices: 90.5 us -> none  [on_device(): clip_cotangent = lax.all_gather(cotangent, 'head', axis=0, tiled=True)]
    pallas_call x1, Pallas kernels: 116 us -> 156 us  [clip_call(): pl.pallas_call(clip_kernel, out_shape=(jax.ShapeDtypeStruct((MERGED, GROU...]
    dot_general x4 -> x0, matrix products: 22.2 us -> none  [the longest x1 8.84 us: dot_t(): lax.dot_general(a, b, (((1,), (1,)), ((), ())), preferred_element_type=jn...]
    unnamed x16 -> x2, local copies, waits for them, and re-layouts: 8.03 us -> 3.41 us
  transfers between devices with their start and end apart: 2 -> 0, of which waited for: 2 -> 0; matrix products, arithmetic and copies ran while one was open for 2% -> 0% of each run, Pallas kernels for 0% -> 0%
where the time goes in v2:
time: 162 us
  Pallas kernels  156 us (96%)
  local copies, waits for them, and re-layouts  4.89 us (3%)
    pallas_call x1, Pallas kernels, clip_call(): pl.pallas_call(clip_kernel, out_shape=(jax.ShapeDtypeStruct((MERGED, GROU...  156 us
    unnamed x2, local copies, waits for them, and re-layouts  3.41 us

profile of v2, /device:TPU:5, one launch (start us, length us, event | category | flops | bytes accessed | tf_op | source)
XLA Modules:
  0.0 162.0 jit_solution(7079981510999136569)
XLA Ops:
  1.3 1.5 pad.4.w_in
  2.8 155.9 %shard_map.113 = (bf16[1024,256]{1,0:T(8,128)(2,1)}, f32[96,256]{1,0:T(8,128)}) custom-call(bf16[256,2048]{1,0:T(8,128)(2,1)} %bitcast.12, bf16[256,2048]{1,0:T(8,128)(2,1)} %bitcast.13, bf16[256,2048]{1,0:T(8,128)(2,1)} %bitcast.14, bf16[256,2048]{1,0:T(8,128)(2,1)} %bitcast.15, bf16[256,2048]{1,0:T(8,128)(2,1)} %bitcast.16, bf16[256,2048]{1,0:T(8,128)(2,1)} %bitcast.17, ...), custom_call_target="tpu_custom_call" | custom-call | flops 10000000000 | bytes 9437184 | tf_op jit(solution)/shard_map/pallas_call | solution.py:512
  158.6 1.9 %copy.15 = bf16[1,1024,256]{2,1,0:T(8,128)(2,1)} copy(bf16[1,1024,256]{2,1,0:T(8,128)(2,1)} %bitcast.10) | data formatting | bytes 1048576
  160.5 1.5 copy.16

commit v3 on v2

--- a/solution.py
+++ b/solution.py
@@ -38,7 +38,7 @@
 def clip_kernel(
     q_hbm, k_hbm, tq_hbm, tk_hbm, v_hbm, tv_hbm, vel_hbm, slot_ref, gap_ref, w_in,
     ga_ref, gw_ref,
-    stage, vel, send, recv, send2, own, k2, v2, w_recv, w_own, w_all, tok, full, acc,
+    w_pad, stage, vel, send, recv, send2, own, k2, v2, w_recv, w_own, w_all, tok, full, acc,
     c_send_buf, quarter, g_buf, term, term_sib, rs_buf, rs_recv, fin,
     in_sem, self_sem, a_send, a_recv, p_send, p_recv, f_send, f_recv, w_send, w_rcv, w_self,
     y_send, y_recv, z_send, z_recv, s_send, s_recv, c_send, c_recv, g_send, g_recv,
@@ -47,14 +47,6 @@
     y_lo, z, core, y_hi, x = place()
     dp = lax.axis_index("dp")
     me = y_hi * 4 + x
-
-    loads = []
-    for i, ref in enumerate((q_hbm, k_hbm, tq_hbm, tk_hbm, v_hbm, tv_hbm)):
-        load = pltpu.make_async_copy(ref, stage.at[i], in_sem.at[i])
-        load.start()
-        loads.append(load)
-    vel_load = pltpu.make_async_copy(vel_hbm, vel, in_sem.at[6])
-    vel_load.start()
 
     peers = [((y_hi + dy) % 2) * 4 + (x + dx) % 4 for dx, dy in PEERS]
     sibling = (dp_of(y_lo, z, 1 - core), me)
@@ -84,21 +76,22 @@
     greet(sibling)
     greet(dest)
     greet(source)
-    pl.semaphore_wait(barrier, 25)
+
+    loads = []
+    for i, ref in enumerate((q_hbm, k_hbm, tq_hbm, tk_hbm, v_hbm, tv_hbm)):
+        load = pltpu.make_async_copy(ref, stage.at[i], in_sem.at[i])
+        load.start()
+        loads.append(load)
+    vel_load = pltpu.make_async_copy(vel_hbm, vel, in_sem.at[6])
+    vel_load.start()
+    w_pad[...] = jnp.zeros_like(w_pad)
+    w_pad[:12] = w_in[...]
 
     def remote(src, dst, ssem, rsem, who):
         return pltpu.make_async_remote_copy(
             src_ref=src, dst_ref=dst, send_sem=ssem, recv_sem=rsem,
             device_id=who, device_id_type=MESH,
         )
-
-    w_copies = []
-    for r in range(7):
-        copy = remote(w_in, w_recv.at[me], w_send.at[r], w_rcv.at[r], (dp, peers[r]))
-        copy.start()
-        w_copies.append(copy)
-    w_local = pltpu.make_async_copy(w_in, w_recv.at[me], w_self.at[0])
-    w_local.start()
 
     rows = lax.broadcasted_iota(jnp.int32, (TOK, SRC_DEV), 0)
     select = slot_ref[...] == rows
@@ -109,17 +102,19 @@
     def merge(i):
         loads[i].wait()
 
-        def body(h, carry):
-            col = pl.multiple_of(h * GROUP, GROUP)
+        def body(n, carry):
+            col = pl.multiple_of(n * 4 * GROUP, 4 * GROUP)
             total = jnp.dot(
-                onehot, stage[i, :, pl.ds(col, GROUP)], preferred_element_type=jnp.float32
+                onehot, stage[i, :, pl.ds(col, 4 * GROUP)], preferred_element_type=jnp.float32
             )
             merged = (total * inverse).astype(jnp.bfloat16)
-            send[h, 0, i] = merged[:, :HD]
-            send[h, 1, i] = merged[:, HD:]
+            for h in range(4):
+                for j in range(2):
+                    first = h * GROUP + j * HD
+                    send[4 * n + h, j, i] = merged[:, first : first + HD]
             return carry
 
-        lax.fori_loop(0, 8, body, 0)
+        lax.fori_loop(0, 2, body, 0)
 
     def exchange(r, j, a):
         return remote(
@@ -130,8 +125,17 @@
             (dp, peers[r]),
         )
 
-    for i in range(3):
+    for i in range(6):
         merge(i)
+    pl.semaphore_wait(barrier, 25)
+
+    w_copies = []
+    for r in range(7):
+        copy = remote(w_pad, w_recv.at[me], w_send.at[r], w_rcv.at[r], (dp, peers[r]))
+        copy.start()
+        w_copies.append(copy)
+    w_local = pltpu.make_async_copy(w_pad, w_recv.at[me], w_self.at[0])
+    w_local.start()
 
     for copy in w_copies:
         copy.wait()
@@ -191,27 +195,30 @@
     keep = pltpu.make_async_copy(w_own, own_slot, w_self.at[1])
     keep.start()
 
-    for r in range(7):
-        exchange(r, 0, 0).start()
-    for i in range(3, 6):
-        merge(i)
-    for j, a in ((0, 1), (1, 0), (1, 1)):
-        for r in range(7):
+    def send_merged(j, a, rs):
+        for r in rs:
             exchange(r, j, a).start()
+
+    same_row = (1, 3, 5)
+    other_row = (0, 2, 4, 6)
+    for j in range(2):
+        for a in range(2):
+            send_merged(j, a, same_row)
     selfs = []
     for j in range(2):
         copy = pltpu.make_async_copy(send.at[me, j], recv.at[j, me], self_sem.at[j])
         copy.start()
         selfs.append(copy)
 
-    other = slot(1, z)
-    remote(other, other, y_send.at[0], y_recv.at[0], partner).wait_recv()
-    ring(0, 0, 1, other, z)
-    ring(1, 0, 1, other, z)
-    to_sibling(other, other)
-
-    def ring_step(step, b):
-        for way in range(2):
+    def from_partner():
+        other = slot(1, z)
+        remote(other, other, y_send.at[0], y_recv.at[0], partner).wait_recv()
+        ring(0, 0, 1, other, z)
+        ring(1, 0, 1, other, z)
+        to_sibling(other, other)
+
+    def ring_step(step, b, ways=(0, 1)):
+        for way in ways:
             if step == 4 and way != b:
                 continue
             ref, plane = landed(way, step, b)
@@ -277,8 +284,6 @@
     def hand_out(j):
         for r in range(7):
             back(r, j).start()
-        for dx in (1, 3, 2):
-            along(dx, j).start()
         col = pl.multiple_of(me * GROUP + j * HD, HD)
         copy = pltpu.make_async_copy(send2.at[j, me], tok.at[:, pl.ds(col, HD)], self_sem.at[2 + j])
         copy.start()
@@ -288,18 +293,30 @@
         copy.start()
         locals_.append(copy)
 
+    def hand_along(j):
+        for dx in (1, 3, 2):
+            along(dx, j).start()
+
+    from_partner()
+    send_merged(0, 0, other_row)
+    send_merged(0, 1, other_row)
     ring_step(1, 0)
-    ring_step(1, 1)
+    send_merged(1, 0, other_row)
+    ring_step(2, 0)
+    send_merged(1, 1, other_row)
     attend(0)
     hand_out(0)
-    ring_step(2, 0)
-    ring_step(2, 1)
+    hand_along(0)
+    ring_step(1, 1)
+    ring_step(3, 0)
     attend(1)
     hand_out(1)
+    ring_step(2, 1)
     vel_load.wait()
     for j in range(2):
         for r in range(7):
             back(r, j).wait_recv()
+    hand_along(1)
     for copy in locals_:
         copy.wait()
     keep.wait()
@@ -355,15 +372,18 @@
             else:
                 acc[...] += part
 
-    from_sibling(6)
+    early = (near % 2 + (near // 2 + x) % 2) % 2
+    halves = (early, 1 - early)
+
+    from_sibling(8)
     project(0)
-    from_sibling(10)
+    ring_step(4, 0)
+    ring_step(3, 1, (1,))
+    from_sibling(12)
     project(1)
-    ring_step(3, 0)
-    ring_step(3, 1)
-    from_sibling(14)
+    ring_step(3, 1, (0,))
+    from_sibling(15)
     project(2)
-    ring_step(4, 0)
     ring_step(4, 1)
     from_sibling(16)
     project(3)
@@ -382,9 +402,6 @@
         g_buf.at[me], ga_ref.at[pl.ds(pl.multiple_of(me * TOK, TOK), TOK)], self_sem.at[8]
     )
     ga_own.start()
-
-    early = (near % 2 + (near // 2 + x) % 2) % 2
-    halves = (early, 1 - early)
 
     def half_term(half):
         for way in range(2):
@@ -448,10 +465,10 @@
     for dx in (1, 3, 2):
         for j in range(2):
             along(dx, j).wait_recv()
-    for half in halves:
-        half_term(half)
-    for half in halves:
-        spread(half)
+    half_term(halves[0])
+    spread(halves[0])
+    half_term(halves[1])
+    spread(halves[1])
 
     for rel in range(1, 16):
         remote(
@@ -518,6 +535,7 @@
         in_specs=[any_spec] * 7 + [vmem, pl.BlockSpec(memory_space=pltpu.SMEM), vmem],
         out_specs=(vmem, vmem),
         scratch_shapes=[
+            pltpu.VMEM((16, F), bf),
             pltpu.VMEM((6, SRC_DEV, F), bf),
             pltpu.VMEM((SRC_DEV, D), bf),
             pltpu.VMEM((8, 2, 6, TOK, HD), bf),
@@ -586,7 +604,7 @@
 ):
     grad_attn, grad_weight = clip_call(
         queries[0], key_states[0], queries_dot[0], keys_dot[0], value_states[0], values_dot[0],
-        velocity[0], merge_slot, time_gap.reshape(1, 1), jnp.pad(out_weight, ((0, 4), (0, 0))),
+        velocity[0], merge_slot, time_gap.reshape(1, 1), out_weight,
     )
     return (grad_attn[None], grad_weight)
 

time: 162 us -> 143 us (0.88)
  Pallas kernels: 156 us -> 138 us
    pallas_call x1, Pallas kernels: 156 us -> 138 us  [clip_call(): pl.pallas_call(clip_kernel, out_shape=(jax.ShapeDtypeStruct((MERGED, GROU...]
where the time goes in v3:
time: 143 us
  Pallas kernels  138 us (97%)
  local copies, waits for them, and re-layouts  3.41 us (2%)
    pallas_call x1, Pallas kernels, clip_call(): pl.pallas_call(clip_kernel, out_shape=(jax.ShapeDtypeStruct((MERGED, GROU...  138 us
    unnamed x2, local copies, waits for them, and re-layouts  3.41 us

profile of v3, /device:TPU:5, one launch (start us, length us, event | category | flops | bytes accessed | tf_op | source)
XLA Modules:
  0.0 142.9 jit_solution(465338570430961802)
XLA Ops:
  1.3 138.2 %shard_map.113 = (bf16[1024,256]{1,0:T(8,128)(2,1)}, f32[96,256]{1,0:T(8,128)}) custom-call(bf16[256,2048]{1,0:T(8,128)(2,1)} %bitcast.12, bf16[256,2048]{1,0:T(8,128)(2,1)} %bitcast.13, bf16[256,2048]{1,0:T(8,128)(2,1)} %bitcast.14, bf16[256,2048]{1,0:T(8,128)(2,1)} %bitcast.15, bf16[256,2048]{1,0:T(8,128)(2,1)} %bitcast.16, bf16[256,2048]{1,0:T(8,128)(2,1)} %bitcast.17, ...), custom_call_target="tpu_custom_call" | custom-call | flops 10000000000 | bytes 9437184 | tf_op jit(solution)/shard_map/pallas_call | solution.py:529
  139.5 1.9 %copy.15 = bf16[1,1024,256]{2,1,0:T(8,128)(2,1)} copy(bf16[1,1024,256]{2,1,0:T(8,128)(2,1)} %bitcast.10) | data formatting | bytes 1048576
  141.3 1.5 %copy.16 = f32[96,256]{1,0:T(8,128)} copy(f32[96,256]{1,0:T(8,128)} %get-tuple-element.9) | data formatting | bytes 196608

commit v4 on v3

--- a/solution.py
+++ b/solution.py
@@ -533,7 +533,7 @@
             jax.ShapeDtypeStruct((ROWS, GROUP), f32),
         ),
         in_specs=[any_spec] * 7 + [vmem, pl.BlockSpec(memory_space=pltpu.SMEM), vmem],
-        out_specs=(vmem, vmem),
+        out_specs=(any_spec, any_spec),
         scratch_shapes=[
             pltpu.VMEM((16, F), bf),
             pltpu.VMEM((6, SRC_DEV, F), bf),

time: 143 us -> 142 us (level)
  no operation moved by 1% of the time
where the time goes in v4:
time: 142 us
  Pallas kernels  137 us (96%)
  local copies, waits for them, and re-layouts  3.41 us (2%)
    pallas_call x1, Pallas kernels, clip_call(): pl.pallas_call(clip_kernel, out_shape=(jax.ShapeDtypeStruct((MERGED, GROU...  137 us
    unnamed x2, local copies, waits for them, and re-layouts  3.41 us

profile of v4, /device:TPU:5, one launch (start us, length us, event | category | flops | bytes accessed | tf_op | source)
XLA Modules:
  0.0 142.0 jit_solution(15513761467933397222)
XLA Ops:
  1.3 137.3 %shard_map.113 = (bf16[1024,256]{1,0:T(8,128)(2,1)}, f32[96,256]{1,0:T(8,128)}) custom-call(bf16[256,2048]{1,0:T(8,128)(2,1)} %bitcast.12, bf16[256,2048]{1,0:T(8,128)(2,1)} %bitcast.13, bf16[256,2048]{1,0:T(8,128)(2,1)} %bitcast.14, bf16[256,2048]{1,0:T(8,128)(2,1)} %bitcast.15, bf16[256,2048]{1,0:T(8,128)(2,1)} %bitcast.16, bf16[256,2048]{1,0:T(8,128)(2,1)} %bitcast.17, ...), custom_call_target="tpu_custom_call" | custom-call | flops 10000000000 | bytes 9437184 | tf_op jit(solution)/shard_map/pallas_call | solution.py:529
  138.5 1.9 %copy.15 = bf16[1,1024,256]{2,1,0:T(8,128)(2,1)} copy(bf16[1,1024,256]{2,1,0:T(8,128)(2,1)} %bitcast.10) | data formatting | bytes 1048576
  140.4 1.5 %copy.16 = f32[96,256]{1,0:T(8,128)} copy(f32[96,256]{1,0:T(8,128)} %get-tuple-element.9) | data formatting | bytes 196608

commit v5 on v4

--- a/solution.py
+++ b/solution.py
@@ -39,7 +39,7 @@
     q_hbm, k_hbm, tq_hbm, tk_hbm, v_hbm, tv_hbm, vel_hbm, slot_ref, gap_ref, w_in,
     ga_ref, gw_ref,
     w_pad, stage, vel, send, recv, send2, own, k2, v2, w_recv, w_own, w_all, tok, full, acc,
-    c_send_buf, quarter, g_buf, term, term_sib, rs_buf, rs_recv, fin,
+    c_send_buf, quarter, g_buf, term, term_out, term_sib, rs_buf, rs_recv, fin,
     in_sem, self_sem, a_send, a_recv, p_send, p_recv, f_send, f_recv, w_send, w_rcv, w_self,
     y_send, y_recv, z_send, z_recv, s_send, s_recv, c_send, c_recv, g_send, g_recv,
     b_send, b_recv, r_send, r_recv, e_send, e_recv,
@@ -424,12 +424,13 @@
                 for c in range(2):
                     top = zi * 192 + c * ROWS
                     term[half, c, zi, block] = part[top : top + ROWS]
+                    term_out[half, c, zi, block] = part[top : top + ROWS].astype(jnp.bfloat16)
         copy = swap(half)
         copy.start()
 
     def swap(half):
         return remote(
-            term.at[half, 1 - core], term_sib.at[half], b_send.at[half], b_recv.at[half], sibling
+            term_out.at[half, 1 - core], term_sib.at[half], b_send.at[half], b_recv.at[half], sibling
         )
 
     def reduce_copy(half, dz):
@@ -448,7 +449,7 @@
         for dz in (4, 3, 5, 2, 6, 1, 7, 0):
             lo, zi, block, copy = reduce_copy(half, dz)
             rs_buf[half, zi, block] = (
-                term[half, core, zi, block] + term_sib[half, zi, block]
+                term[half, core, zi, block] + term_sib[half, zi, block].astype(jnp.float32)
             ).astype(jnp.bfloat16)
             if dz:
                 copy.start()
@@ -554,7 +555,8 @@
             pltpu.VMEM((2, 384, MERGED), bf),
             pltpu.VMEM((8, TOK, GROUP), bf),
             pltpu.VMEM((2, 2, 2, 4, ROWS, GROUP), f32),
-            pltpu.VMEM((2, 2, 4, ROWS, GROUP), f32),
+            pltpu.VMEM((2, 2, 2, 4, ROWS, GROUP), bf),
+            pltpu.VMEM((2, 2, 4, ROWS, GROUP), bf),
             pltpu.VMEM((2, 2, 4, ROWS, GROUP), bf),
             pltpu.VMEM((16, ROWS, GROUP), bf),
             pltpu.VMEM((ROWS, GROUP), f32),

time: 142 us -> 143 us (level)
  no operation moved by 1% of the time
where the time goes in v5:
time: 143 us; the launch traced here: 142 us
  Pallas kernels  138 us (97%)
  local copies, waits for them, and re-layouts  3.41 us (2%)
    pallas_call x1, Pallas kernels, clip_call(): pl.pallas_call(clip_kernel, out_shape=(jax.ShapeDtypeStruct((MERGED, GROU...  138 us
    unnamed x2, local copies, waits for them, and re-layouts  3.41 us

profile of v5, /device:TPU:5, one launch (start us, length us, event | category | flops | bytes accessed | tf_op | source)
XLA Modules:
  0.0 142.4 jit_solution(2526531936927802552)
XLA Ops:
  1.3 137.7 %shard_map.113 = (bf16[1024,256]{1,0:T(8,128)(2,1)}, f32[96,256]{1,0:T(8,128)}) custom-call(bf16[256,2048]{1,0:T(8,128)(2,1)} %bitcast.12, bf16[256,2048]{1,0:T(8,128)(2,1)} %bitcast.13, bf16[256,2048]{1,0:T(8,128)(2,1)} %bitcast.14, bf16[256,2048]{1,0:T(8,128)(2,1)} %bitcast.15, bf16[256,2048]{1,0:T(8,128)(2,1)} %bitcast.16, bf16[256,2048]{1,0:T(8,128)(2,1)} %bitcast.17, ...), custom_call_target="tpu_custom_call" | custom-call | flops 10000000000 | bytes 9437184 | tf_op jit(solution)/shard_map/pallas_call | solution.py:530
  139.0 1.9 %copy.15 = bf16[1,1024,256]{2,1,0:T(8,128)(2,1)} copy(bf16[1,1024,256]{2,1,0:T(8,128)(2,1)} %bitcast.10) | data formatting | bytes 1048576
  140.9 1.5 %copy.16 = f32[96,256]{1,0:T(8,128)} copy(f32[96,256]{1,0:T(8,128)} %get-tuple-element.9) | data formatting | bytes 196608
